TPU v7x, 32 devices: a whole 2x2x4 slice. The times are simulated.
32 devices in a mesh: groups: 2 (over y), dp: 4 (over x, core), tensor: 4 (over z).
Axes of the slice: x: 2, y: 2, z: 4, core: 2. Of those that a mesh axis runs over, the one named last changes fastest.
Arguments:
- queries: bfloat16 [640, 16384], P(('groups', 'dp'), 'tensor'), parts along dimension 0, may hold values from -8 to 8, as said below
- kv_pool: bfloat16 [80, 8, 64, 256], P(('groups', 'dp')), parts along dimension 0, may hold values from -8 to 8, as said below
- out_weight: bfloat16 [16384, 16384], P('tensor', 'dp'), may hold values from -0.046875 to 0.046875
- residual: bfloat16 [640, 16384], P(('groups', 'tensor'), 'dp'), parts along dimension 0, may hold values from -1.5 to 1.5
- block_lists: int32 [640, 8], P(('groups', 'dp')), parts along dimension 0, may hold values from 0 to 39, as said below
- lengths: int32 [640], P(('groups', 'dp')), parts along dimension 0, may hold values from 1 to 512, as said below
Outputs:
- mixed: bfloat16 [640, 16384], P(('groups', 'tensor'), 'dp'), parts along dimension 0
There are 2 independent parts, one for each index of `groups`. A program takes and returns all parts, laid end to end along the dimension named above; an argument that names none is the same for every part. Nothing has to cross between parts.
Inputs may be any that keep to these rules, and one draw needn't show every extreme that they name: The values of the queries and of the cached keys and values lie in this range. `kv_pool`: as for queries. `block_lists`: each row names 8 distinct blocks, 2 stored on each index of dp. The rows of one index of dp (aligned blocks of 80 rows) name exactly 4 distinct blocks stored on each index of dp. `lengths`: some row has the full length.
All inputs are finite; a program needn't handle non-finite values.
Results may differ from a plain program's by a relative error of at most 0.01.
Values may be sent and summed in bfloat16 or wider, within the bound.
A program may use at most 192 MiB of HBM per device.

v0:
```python
import math

import jax
import jax.numpy as jnp
from jax import lax
from jax.sharding import PartitionSpec as P


def attend_blocks(state_in, query_heads, block_ids, block_data, block_lists, lengths, head_dim):
    row_max, row_total, accumulated = state_in
    block_len = block_data.shape[2]
    list_len = block_lists.shape[1]
    matches = block_lists[:, :, None] == block_ids[None, None, :]
    named_any = jnp.any(matches, axis=1)
    position = jnp.sum(
        matches.astype(jnp.int32) * jnp.arange(list_len, dtype=jnp.int32)[None, :, None], axis=1
    )
    offsets = (
        position[:, :, None] * block_len + jnp.arange(block_len, dtype=jnp.int32)[None, None, :]
    )
    visible = named_any[:, :, None] & (offsets < lengths[:, None, None])
    key_part = block_data[..., :head_dim]
    value_part = block_data[..., head_dim:]
    scores = jnp.einsum(
        "rkqd,nkbd->rkqnb", query_heads, key_part, preferred_element_type=jnp.float32
    ) / math.sqrt(head_dim)
    visible_full = visible[:, None, None, :, :]
    piece_max = jnp.max(jnp.where(visible_full, scores, -1e30), axis=(3, 4))
    new_max = jnp.maximum(row_max, piece_max)
    weights = jnp.where(visible_full, jnp.exp(scores - new_max[..., None, None]), 0.0)
    row_total = jnp.sum(weights, axis=(3, 4))
    accumulated = jnp.einsum(
        "rkqnb,nkbd->rkqd",
        weights.astype(jnp.bfloat16),
        value_part,
        preferred_element_type=jnp.float32,
    )
    return (new_max, row_total, accumulated)


def on_device(queries, kv_pool, out_weight, residual, block_lists, lengths):
    tensor_size = lax.axis_size("tensor")
    row_count, query_width = queries.shape
    store_count, kv_heads, block_len, pair_width = kv_pool.shape
    head_dim = pair_width // 2
    local_heads = query_width // head_dim
    head_group = local_heads * tensor_size // kv_heads
    local_kv = max(1, local_heads // head_group)
    first_kv = lax.axis_index("tensor") * local_heads // head_group
    own_pool = lax.dynamic_slice_in_dim(kv_pool, first_kv, local_kv, 1)
    query_heads = queries.reshape(row_count, local_kv, local_heads // local_kv, head_dim)
    state_shape = (row_count, local_kv, local_heads // local_kv)
    start_state = (
        jnp.full(state_shape, -1e30, jnp.float32),
        jnp.zeros(state_shape, jnp.float32),
        jnp.zeros(state_shape + (head_dim,), jnp.float32),
    )
    shard_blocks = lax.all_gather(own_pool, "dp", axis=0, tiled=True)
    block_ids = jnp.arange(shard_blocks.shape[0], dtype=jnp.int32)
    final_state = attend_blocks(
        start_state, query_heads, block_ids, shard_blocks, block_lists, lengths, head_dim
    )
    row_max, row_total, accumulated = final_state
    attended = (
        (accumulated / row_total[..., None]).astype(jnp.bfloat16).reshape(row_count, query_width)
    )
    partial_value = jnp.dot(
        lax.all_gather(attended, "dp", axis=0, tiled=True),
        out_weight,
        preferred_element_type=jnp.float32,
    )
    summed = lax.psum_scatter(
        partial_value.astype(jnp.bfloat16), "tensor", scatter_dimension=0, tiled=True
    ).astype(jnp.float32)
    return (residual.astype(jnp.float32) + summed).astype(jnp.bfloat16)


def solution(mesh):
    in_specs = (
        P(("groups", "dp"), "tensor"),
        P(("groups", "dp"), None, None, None),
        P("tensor", "dp"),
        P(("groups", "tensor"), "dp"),
        P(("groups", "dp"), None),
        P(("groups", "dp")),
    )
    out_specs = P(("groups", "tensor"), "dp")
    return jax.shard_map(
        on_device, mesh=mesh, in_specs=in_specs, out_specs=out_specs, check_vma=False
    )
```

profile of v0, /device:TPU:2, one launch (start us, length us, event | category | flops | bytes accessed | tf_op | source)
XLA Modules:
  0.0 196.6 jit_solution(901615525600784632)
XLA Ops:
  6.5 0.0 copy-start
  6.5 0.0 all-gather.3.cloned.1.call-start
  6.5 1.7 copy-done
  8.3 0.1 constant_dynamic-slice_fusion
  8.3 0.9 copy.26
  9.2 0.0 all-gather.3.cloned.1.call-update
  9.3 0.0 all-gather.5.cloned.1.call-start
  9.3 1.2 copy.27
  10.5 0.7 fusion.16
  11.2 0.7 select_reduce_fusion
  12.0 1.0 fusion.12
  13.0 22.1 %all-gather.3.cloned.1.call-done = bf16[40,2,64,256]{3,2,0,1:T(8,128)(2,1)} async-done(((bf16[10,2,64,256]{3,2,0,1:T(8,128)(2,1)}), bf16[40,2,64,256]{3,2,0,1:T(8,128)(2,1)}) %all-gather.3.cloned.1.call-update) | async-done | bytes 2621456 | tf_op jit(solution)/shard_map/all_gather | solution.py:58
  35.0 18.7 %fusion = (f32[80,2,16]{0,2,1:T(8,128)S(1)}, f32[2,40,64,80,16]{3,2,4,1,0:T(8,128)}) fusion(pred[80,40,64]{0,2,1:T(8,128)(4,1)S(1)} %fusion.12, bf16[80,2,16,128,1]{3,2,1,0,4:T(8,128)(2,1)S(1)} %bitcast.55, bf16[40,2,64,256]{3,2,0,1:T(8,128)(2,1)} %all-gather.3.cloned.1.call-done), kind=kOutput, calls=%fused_computation.2 | convolution fusion | flops 1697379840 | bytes 28395520 | tf_op jit(solution)/shard_map/rkqd,nkbd->rkqnb/dot_general | solution.py:24
  53.7 0.0 copy-start.2
  53.7 18.2 %fusion.3 = f32[80,2,16]{0,2,1:T(8,128)S(1)} fusion(f32[2,40,64,80,16]{3,2,4,1,0:T(8,128)} %get-tuple-element.6, f32[80,2,16]{0,2,1:T(8,128)S(1)} %broadcast_maximum_fusion, pred[80,40,64]{0,2,1:T(8,128)(4,1)S(1)} %fusion.12), kind=kLoop, calls=%fused_computation.5 | loop fusion | flops 26211840 | bytes 26439680 | tf_op jit(solution)/shard_map/reduce_sum | solution.py:31
  71.9 0.0 copy-done.2
  71.9 16.7 %divide_convert_fusion = bf16[80,2,16,128]{3,0,2,1:T(8,128)(2,1)S(1)} fusion(f32[2,40,64,80,16]{3,2,4,1,0:T(8,128)} %get-tuple-element.6, f32[80,2,16]{0,2,1:T(8,128)S(1)} %broadcast_maximum_fusion, pred[80,40,64]{0,2,1:T(8,128)(4,1)S(1)} %fusion.12, bf16[40,2,64,256]{3,2,0,1:T(8,128)(2,1)S(1)} %copy-done.2, f32[80,2,16]{0,2,1:T(8,128)S(1)} %fusion.3), kind=kOutput, calls=%fused_computation.15 | convolution fusion | flops 1704591360 | bytes 28540928 | tf_op jit(solution)/shard_map/rkqnb,nkbd->rkqd/dot_general | solution.py:32
  88.6 0.2 copy.19
  88.8 1.1 copy.34
  89.9 0.0 all-gather.5.cloned.1.call-update
  89.9 0.0 copy-start.3
  89.9 0.2 reduce-scatter.2.cloned.1.call-start
  90.2 25.5 %all-gather.5.cloned.1.call-done = bf16[320,4096]{1,0:T(8,128)(2,1)} async-done(((bf16[80,4096]{1,0:T(8,128)(2,1)}), bf16[320,4096]{1,0:T(8,128)(2,1)}) %all-gather.5.cloned.1.call-update) | async-done | bytes 2621456 | tf_op jit(solution)/shard_map/all_gather | solution.py:68
  115.6 0.0 copy-start.1
  115.6 18.9 %convolution_convert_fusion = bf16[320,4096]{1,0:T(8,128)(2,1)} fusion(bf16[320,4096]{1,0:T(8,128)(2,1)} %all-gather.5.cloned.1.call-done, bf16[4096,4096]{1,0:T(8,128)(2,1)} %param.8), kind=kOutput, calls=%fused_computation.9 | convolution fusion | flops 10738728960 | bytes 38797312 | tf_op jit(solution)/shard_map/dot_general | solution.py:67
  134.5 0.0 reduce-scatter.2.cloned.1.call-update
  134.5 53.4 %reduce-scatter.2.cloned.1.call-done = bf16[80,4096]{1,0:T(8,128)(2,1)} async-done(((bf16[320,4096]{1,0:T(8,128)(2,1)}), bf16[80,4096]{1,0:T(8,128)(2,1)}) %reduce-scatter.2.cloned.1.call-update) | async-done | bytes 655376 | tf_op jit(solution)/shard_map/reduce_scatter | solution.py:72
  188.0 0.0 copy-done.3
  188.0 2.1 %add_convert_fusion = bf16[80,4096]{1,0:T(8,128)(2,1)} fusion(bf16[80,4096]{1,0:T(8,128)(2,1)} %reduce-scatter.2.cloned.1.call-done, bf16[80,4096]{1,0:T(8,128)(2,1)S(1)} %copy-done.3), kind=kLoop, calls=%fused_computation.14 | loop fusion | flops 1310720 | bytes 1966080 | tf_op jit(solution)/shard_map/convert_element_type | solution.py:75
  190.0 0.0 copy-done.1
  (2 shorter events, 0.0 us)
Async XLA Ops:
  6.5 1.7 copy-start
  6.5 28.5 %all-gather.3.cloned.1.call-start = ((), (), s32[]{:S(2)}) async-start(), calls=%async_computation.1 | async-start | bytes 3276800 | tf_op jit(solution)/shard_map/all_gather | solution.py:58
  9.3 106.4 %all-gather.5.cloned.1.call-start = ((), (), s32[]{:S(2)}) async-start(), calls=%async_computation.2 | async-start | bytes 3276800 | tf_op jit(solution)/shard_map/all_gather | solution.py:68
  53.7 18.2 %copy-start.2 = (bf16[40,2,64,256]{3,2,0,1:T(8,128)(2,1)S(1)}, bf16[40,2,64,256]{3,2,0,1:T(8,128)(2,1)}, u32[]{:S(2)}) copy-start(bf16[40,2,64,256]{3,2,0,1:T(8,128)(2,1)} %all-gather.3.cloned.1.call-done) | copy-start | bytes 7864324
  89.9 98.0 %copy-start.3 = (bf16[80,4096]{1,0:T(8,128)(2,1)S(1)}, bf16[80,4096]{1,0:T(8,128)(2,1)}, u32[]{:S(2)}) copy-start(bf16[80,4096]{1,0:T(8,128)(2,1)} %param.9) | copy-start | bytes 1966084
  89.9 98.0 %reduce-scatter.2.cloned.1.call-start = ((), (), s32[]{:S(2)}) async-start(), calls=%async_computation.3 | async-start | bytes 3276800 | tf_op jit(solution)/shard_map/reduce_scatter | solution.py:72
  115.6 74.4 %copy-start.1 = (bf16[10,8,64,256]{3,2,1,0:T(8,128)(2,1)S(1)}, bf16[10,8,64,256]{3,2,1,0:T(8,128)(2,1)}, u32[]{:S(2)}) copy-start(bf16[10,8,64,256]{3,2,1,0:T(8,128)(2,1)} %param.7) | copy-start | bytes 7864324
Sparse Core Ops, SparseCore 0:
  9.4 25.6 all-gather.2
  90.0 25.5 all-gather.4
  134.7 53.2 reduce-scatter.1
where the time goes:
time: 199 us; the launch traced here: 197 us
  waiting for transfers between devices  101 us (51%)
  matrix products  54.3 us (27%)
  other arithmetic  22.7 us (11%)
  between operations  13.2 us (7%)
  local copies, waits for them, and re-layouts  5.18 us (3%)
    reduce_scatter x1, waiting for transfers between devices, on_device(): lax.psum_scatter(partial_value.astype(jnp.bfloat16), 'tensor', scatter_di...  53.4 us
    all_gather x1, waiting for transfers between devices, on_device(): lax.all_gather(attended, 'dp', axis=0, tiled=True)  25.5 us
    all_gather x1, waiting for transfers between devices, on_device(): shard_blocks = lax.all_gather(own_pool, 'dp', axis=0, tiled=True)  22.1 us
    dot_general x1, matrix products, on_device(): jnp.dot(lax.all_gather(attended, 'dp', axis=0, tiled=True), out_weight, p...  18.9 us
    dot_general x1, matrix products, attend_blocks(): jnp.einsum('rkqd,nkbd->rkqnb', query_heads, key_part, preferred_element_t...  18.7 us
    reduce_sum x1, other arithmetic, attend_blocks(): row_total = jnp.sum(weights, axis=(3, 4))  18.2 us
    dot_general x1, matrix products, attend_blocks(): jnp.einsum('rkqnb,nkbd->rkqd', weights.astype(jnp.bfloat16), value_part,...  16.7 us
    unnamed x11, local copies, waits for them, and re-layouts  4.96 us
  transfers between devices with their start and end apart: 3, of which 3 were waited for; matrix products, arithmetic and copies ran while one was open for 2% of the time, Pallas kernels for 0%

commit v1 on v0

--- a/solution.py
+++ b/solution.py
@@ -3,6 +3,8 @@
 import jax
 import jax.numpy as jnp
 from jax import lax
+from jax.experimental import pallas as pl
+from jax.experimental.pallas import tpu as pltpu
 from jax.sharding import PartitionSpec as P
 
 
@@ -38,7 +40,7 @@
     return (new_max, row_total, accumulated)
 
 
-def on_device(queries, kv_pool, out_weight, residual, block_lists, lengths):
+def generic_device(queries, kv_pool, out_weight, residual, block_lists, lengths):
     tensor_size = lax.axis_size("tensor")
     row_count, query_width = queries.shape
     store_count, kv_heads, block_len, pair_width = kv_pool.shape
@@ -75,6 +77,344 @@
     return (residual.astype(jnp.float32) + summed).astype(jnp.bfloat16)
 
 
+MESH = pl.DeviceIdType.MESH
+CAP = 4
+CHUNK = 512
+
+
+def fused_kernel(
+    q_ref, kv_ref, w_ref, res_ref, bl_ref, len_ref, out_ref,
+    w_v, kvb, kc, vc, bias, ids_v, ids_s, attb, stg, rl, rr, facc,
+    w_sem, ids_sem, kvl_sem, kv_send, kv_recv, at_send, at_recv, z_send, zl_recv, zr_recv,
+):
+    rows, width = q_ref.shape
+    stores, kv_heads, blk, pair = kv_ref.shape
+    hd = pair // 2
+    n_dp, nz = attb.shape[0], stg.shape[0]
+    slots = CAP * n_dp
+    local_heads = width // hd
+    local_kv = len(kvb) // 2
+    head_group = local_heads // local_kv
+    per = CHUNK // hd
+    groups_per_kv = head_group // per
+    n_att = width // CHUNK
+    n_col = w_v.shape[0]
+    d = lax.axis_index("dp")
+    z = lax.axis_index("tensor")
+    x, c = d // 2, d % 2
+    mate = 2 * x + (1 - c)
+    across = 2 * (1 - x) + c
+    diag = 2 * (1 - x) + (1 - c)
+
+    def w_copy(j):
+        cols = pl.ds(pl.multiple_of(j * CHUNK, CHUNK), CHUNK)
+        return pltpu.make_async_copy(w_ref.at[:, cols], w_v.at[j], w_sem.at[j])
+
+    def kv_src(t):
+        return kv_ref.at[:, z * local_kv + t // 2, :, pl.ds((t % 2) * hd, hd)]
+
+    def kv_dst(t, owner):
+        return kvb[t].at[pl.ds(owner * stores, stores)]
+
+    def kv_local(t):
+        return pltpu.make_async_copy(kv_src(t), kv_dst(t, d), kvl_sem.at[t])
+
+    def kv_remote(kind, t):
+        owner = across if kind == 2 else d
+        src = kv_dst(t, owner) if kind == 2 else kv_src(t)
+        return pltpu.make_async_remote_copy(
+            src_ref=src, dst_ref=kv_dst(t, owner),
+            send_sem=kv_send.at[kind, t], recv_sem=kv_recv.at[kind, t],
+            device_id={"dp": across if kind == 1 else mate}, device_id_type=MESH,
+        )
+
+    def att_remote(kind, i):
+        owner = across if kind == 2 else d
+        cols = pl.ds(pl.multiple_of(i * CHUNK, CHUNK), CHUNK)
+        ref = attb.at[owner, :, cols]
+        return pltpu.make_async_remote_copy(
+            src_ref=ref, dst_ref=ref,
+            send_sem=at_send.at[kind, i], recv_sem=at_recv.at[kind, i],
+            device_id={"dp": across if kind == 1 else mate}, device_id_type=MESH,
+        )
+
+    def z_remote(b, j, right):
+        cols = pl.ds(pl.multiple_of(j * CHUNK, CHUNK), CHUNK)
+        land, sem = (rl, zl_recv) if right else (rr, zr_recv)
+        return pltpu.make_async_remote_copy(
+            src_ref=stg.at[b, :, cols], dst_ref=land.at[b, :, cols],
+            send_sem=z_send.at[b, j], recv_sem=sem.at[b, j],
+            device_id={"tensor": z + 1 if right else z - 1}, device_id_type=MESH,
+        )
+
+    for t in range(2 * local_kv):
+        kv_local(t).start()
+    for j in range(n_col):
+        w_copy(j).start()
+
+    barrier = pltpu.get_barrier_semaphore()
+    pl.semaphore_signal(barrier, inc=1, device_id={"dp": mate}, device_id_type=MESH)
+    pl.semaphore_signal(barrier, inc=1, device_id={"dp": across}, device_id_type=MESH)
+
+    @pl.when(z > 0)
+    def _():
+        pl.semaphore_signal(barrier, inc=1, device_id={"tensor": z - 1}, device_id_type=MESH)
+
+    @pl.when(z < nz - 1)
+    def _():
+        pl.semaphore_signal(barrier, inc=1, device_id={"tensor": z + 1}, device_id_type=MESH)
+
+    pl.semaphore_wait(
+        barrier, 2 + (z > 0).astype(jnp.int32) + (z < nz - 1).astype(jnp.int32)
+    )
+
+    for t in range(2 * local_kv):
+        kv_remote(1, t).start()
+    for t in range(2 * local_kv):
+        kv_remote(0, t).start()
+
+    bl = bl_ref[...]
+    list_len = bl.shape[1]
+    lane = lax.broadcasted_iota(jnp.int32, (rows, 128), 1)
+    hit = jnp.zeros((rows, 128), jnp.int32)
+    for k in range(list_len):
+        hit = jnp.maximum(hit, (bl[:, k : k + 1] == lane).astype(jnp.int32))
+    named_l = jnp.max(hit, axis=0, keepdims=True)
+    sub2 = lax.broadcasted_iota(jnp.int32, (128, 128), 0)
+    lane2 = lax.broadcasted_iota(jnp.int32, (128, 128), 1)
+    named_b = jnp.broadcast_to(named_l, (128, 128))
+    named_s = jnp.sum(jnp.where(sub2 == lane2, named_b, 0), axis=1, keepdims=True)
+    rank = jnp.sum(jnp.where(lane2 < sub2, named_b, 0), axis=1, keepdims=True)
+    picked = jnp.where((rank == lane2) & (named_s > 0), sub2, 0)
+    ids = jnp.sum(picked, axis=0, keepdims=True)
+    ids_v[...] = jnp.broadcast_to(ids, ids_v.shape)
+    ids_copy = pltpu.make_async_copy(ids_v, ids_s, ids_sem)
+    ids_copy.start()
+    ids_copy.wait()
+
+    eye_r = lax.broadcasted_iota(jnp.int32, (rows, rows), 0)
+    eye_c = lax.broadcasted_iota(jnp.int32, (rows, rows), 1)
+    len_b = jnp.broadcast_to(len_ref[...], (rows, rows))
+    length = jnp.sum(jnp.where(eye_r == eye_c, len_b, 0), axis=1, keepdims=True)
+    place = lax.broadcasted_iota(jnp.int32, (rows, list_len), 1)
+    token = lax.broadcasted_iota(jnp.int32, (rows, 2 * blk), 1)
+    for pair_of in range(slots // 2):
+        limits = []
+        for k in range(2):
+            match = bl == ids_s[0, 2 * pair_of + k]
+            left = jnp.where(match, length - place * blk, 0)
+            limits.append(jnp.max(left, axis=1, keepdims=True))
+        limit = jnp.where(token < blk, jnp.minimum(limits[0], blk), limits[1] + blk)
+        bias[:, 2 * blk * pair_of : 2 * blk * (pair_of + 1)] = jnp.where(token < limit, 0.0, -1e30)
+
+    scale = 1.0 / math.sqrt(hd)
+    for h in range(local_kv):
+        for t in (2 * h, 2 * h + 1):
+            kv_remote(1, t).wait_recv()
+            kv_remote(2, t).start()
+        for t in (2 * h, 2 * h + 1):
+            kv_local(t).wait()
+            kv_remote(0, t).wait_recv()
+            kv_remote(2, t).wait_recv()
+        for j in range(slots):
+            pick = ids_s[0, j]
+            kc[blk * j : blk * (j + 1), :] = kvb[2 * h][pick]
+            vc[blk * j : blk * (j + 1), :] = kvb[2 * h + 1][pick]
+
+        @pl.loop(0, groups_per_kv)
+        def _(g):
+            i = h * groups_per_kv + g
+            cols = pl.ds(pl.multiple_of(i * CHUNK, CHUNK), CHUNK)
+            qs = q_ref[:, cols]
+            stacked = jnp.concatenate(
+                [qs[:, hd * k : hd * (k + 1)] for k in range(per)], axis=0
+            )
+            scores = lax.dot_general(
+                stacked, kc[...], (((1,), (1,)), ((), ())), preferred_element_type=jnp.float32
+            ).reshape(per, rows, slots * blk)
+            scores = scores * scale + bias[...][None]
+            top = jnp.max(scores, axis=2, keepdims=True)
+            weights = jnp.exp(scores - top)
+            total = jnp.sum(weights, axis=2, keepdims=True)
+            summed = jnp.dot(
+                weights.astype(jnp.bfloat16).reshape(per * rows, slots * blk),
+                vc[...], preferred_element_type=jnp.float32,
+            ).reshape(per, rows, hd)
+            attended = (summed / total).astype(jnp.bfloat16)
+            attb[d, :, cols] = jnp.concatenate([attended[k] for k in range(per)], axis=1)
+            att_remote(1, i).start()
+            att_remote(0, i).start()
+
+    @pl.loop(0, n_att)
+    def _(i):
+        att_remote(0, i).wait_recv()
+
+    inner = (z > 0) & (z < nz - 1)
+    half = nz // 2
+
+    def block_of(s, i):
+        chip = jnp.where(s < n_col, x, 1 - x)
+        return 2 * chip + jnp.where(z < half, 1 - i, i)
+
+    def send_end(s):
+        j = s % n_col
+        for i in range(2):
+            b = block_of(s, i)
+
+            @pl.when((z == 0) & (b > 0))
+            def _():
+                z_remote(b, j, True).start()
+
+            @pl.when((z == nz - 1) & (b < nz - 1))
+            def _():
+                z_remote(b, j, False).start()
+
+    def send_inner(s):
+        j = s % n_col
+        cols = pl.ds(pl.multiple_of(j * CHUNK, CHUNK), CHUNK)
+
+        def pass_on(b, right):
+            land = rl if right else rr
+            z_remote(b, j, right).wait_recv()
+            added = stg[b, :, cols].astype(jnp.float32) + land[b, :, cols].astype(jnp.float32)
+            stg[b, :, cols] = added.astype(jnp.bfloat16)
+            z_remote(b, j, right).start()
+
+        for i in range(2):
+            b = block_of(s, i)
+
+            @pl.when(inner & (b > z))
+            def _():
+                pass_on(b, True)
+
+            @pl.when(inner & (b < z))
+            def _():
+                pass_on(b, False)
+
+    @pl.loop(0, 2 * n_col)
+    def _(s):
+        j = s % n_col
+        cols = pl.ds(pl.multiple_of(j * CHUNK, CHUNK), CHUNK)
+
+        @pl.when(s < n_col)
+        def _():
+            w_copy(j).wait()
+            att_remote(1, j).wait_recv()
+            att_remote(2, j).start()
+
+        @pl.when(s == n_col)
+        def _():
+            @pl.loop(0, n_att)
+            def _(i):
+                att_remote(2, i).wait_recv()
+
+        chip = jnp.where(s < n_col, x, 1 - x)
+        part = attb[pl.ds(2 * chip, 2)].reshape(2 * rows, width)
+        partial = jnp.dot(part, w_v[j], preferred_element_type=jnp.float32)
+        stg[pl.ds(2 * chip, 2), :, cols] = partial.astype(jnp.bfloat16).reshape(2, rows, CHUNK)
+        send_end(s)
+
+        @pl.when(s > 0)
+        def _():
+            send_inner(s - 1)
+
+    send_inner(2 * n_col - 1)
+
+    @pl.loop(0, n_col)
+    def _(j):
+        cols = pl.ds(pl.multiple_of(j * CHUNK, CHUNK), CHUNK)
+        facc[...] = res_ref[:, cols].astype(jnp.float32) + stg[z, :, cols].astype(jnp.float32)
+
+        @pl.when(z > 0)
+        def _():
+            z_remote(z, j, True).wait_recv()
+            facc[...] += rl[z, :, cols].astype(jnp.float32)
+
+        @pl.when(z < nz - 1)
+        def _():
+            z_remote(z, j, False).wait_recv()
+            facc[...] += rr[z, :, cols].astype(jnp.float32)
+
+        out_ref[:, cols] = facc[...].astype(jnp.bfloat16)
+
+    for kind in range(3):
+        for t in range(2 * local_kv):
+            kv_remote(kind, t).wait_send()
+
+        @pl.loop(0, n_att)
+        def _(i):
+            att_remote(kind, i).wait_send()
+
+    @pl.loop(0, n_col)
+    def _(j):
+        for b in range(nz):
+
+            @pl.when(z < b)
+            def _():
+                z_remote(b, j, True).wait_send()
+
+            @pl.when(z > b)
+            def _():
+                z_remote(b, j, False).wait_send()
+
+
+def fused_device(queries, kv_pool, out_weight, residual, block_lists, lengths):
+    n_dp, nz = lax.axis_size("dp"), lax.axis_size("tensor")
+    rows, width = queries.shape
+    stores, kv_heads, blk, pair = kv_pool.shape
+    hd = pair // 2
+    columns = out_weight.shape[1]
+    local_kv = kv_heads // nz
+    n_att, n_col = width // CHUNK, columns // CHUNK
+    tokens = CAP * n_dp * blk
+    bf16, f32 = jnp.bfloat16, jnp.float32
+    dma = pltpu.SemaphoreType.DMA
+    vmem = pl.BlockSpec(memory_space=pltpu.VMEM)
+    hbm = pl.BlockSpec(memory_space=pl.ANY)
+    return pl.pallas_call(
+        fused_kernel,
+        out_shape=jax.ShapeDtypeStruct((rows, columns), bf16),
+        in_specs=[vmem, hbm, hbm, vmem, vmem, vmem],
+        out_specs=vmem,
+        scratch_shapes=[
+            pltpu.VMEM((n_col, width, CHUNK), bf16),
+            [pltpu.VMEM((n_dp * stores, blk, hd), bf16)] * (2 * local_kv),
+            pltpu.VMEM((tokens, hd), bf16),
+            pltpu.VMEM((tokens, hd), bf16),
+            pltpu.VMEM((rows, tokens), f32),
+            pltpu.VMEM((8, 128), jnp.int32),
+            pltpu.SMEM((8, 128), jnp.int32),
+            pltpu.VMEM((n_dp, rows, width), bf16),
+            pltpu.VMEM((nz, rows, columns), bf16),
+            pltpu.VMEM((nz, rows, columns), bf16),
+            pltpu.VMEM((nz, rows, columns), bf16),
+            pltpu.VMEM((rows, CHUNK), f32),
+            dma((n_col,)),
+            dma,
+            dma((2 * local_kv,)),
+            dma((3, 2 * local_kv)),
+            dma((3, 2 * local_kv)),
+            dma((3, n_att)),
+            dma((3, n_att)),
+            dma((nz, n_col)),
+            dma((nz, n_col)),
+            dma((nz, n_col)),
+        ],
+        compiler_params=pltpu.CompilerParams(
+            collective_id=0, has_side_effects=True, vmem_limit_bytes=60 * 1024 * 1024
+        ),
+        cost_estimate=pl.CostEstimate(
+            flops=2 * n_dp * rows * width * columns,
+            bytes_accessed=2 * width * columns,
+            transcendentals=rows * width // hd * tokens,
+        ),
+    )(queries, kv_pool, out_weight, residual, block_lists, lengths.reshape(1, rows))
+
+
+def fits_fused(mesh):
+    return mesh.shape["dp"] == 4 and mesh.shape["tensor"] == 4
+
+
 def solution(mesh):
     in_specs = (
         P(("groups", "dp"), "tensor"),
@@ -85,6 +425,7 @@
         P(("groups", "dp")),
     )
     out_specs = P(("groups", "tensor"), "dp")
+    body = fused_device if fits_fused(mesh) else generic_device
     return jax.shard_map(
-        on_device, mesh=mesh, in_specs=in_specs, out_specs=out_specs, check_vma=False
-    )
+        body, mesh=mesh, in_specs=in_specs, out_specs=out_specs, check_vma=False
+    )

time: 199 us -> 96.2 us (0.48); the launches traced: 197 us -> 95.9 us
  waiting for transfers between devices: 101 us -> 0 us
  Pallas kernels: 0 us -> 92.6 us
  matrix products: 54.3 us -> 0 us
  other arithmetic: 22.7 us -> 0 us
  between operations: 13.2 us -> 0.01 us
    pallas_call x0 -> x1, Pallas kernels: none -> 92.6 us  [fused_device(): pl.pallas_call(fused_kernel, out_shape=jax.ShapeDtypeStruct((rows, column...]
    dot_general x3 -> x0, matrix products: 54.3 us -> none  [the longest x1 18.9 us: on_device(): jnp.dot(lax.all_gather(attended, 'dp', axis=0, tiled=True), out_weight, p...]
    reduce_scatter x1 -> x0, waiting for transfers between devices: 53.4 us -> none  [on_device(): lax.psum_scatter(partial_value.astype(jnp.bfloat16), 'tensor', scatter_di...]
    all_gather x2 -> x0, waiting for transfers between devices: 47.6 us -> none  [the longest x1 25.5 us: on_device(): lax.all_gather(attended, 'dp', axis=0, tiled=True)]
    reduce_sum x2 -> x0, other arithmetic: 18.9 us -> none  [the longest x1 18.2 us: attend_blocks(): row_total = jnp.sum(weights, axis=(3, 4))]
    convert_element_type x1 -> x0, other arithmetic: 2.08 us -> none  [on_device(): return (residual.astype(jnp.float32) + summed).astype(jnp.bfloat16)]
    unnamed x11 -> x2, local copies, waits for them, and re-layouts: 4.96 us -> 3.36 us
  transfers between devices with their start and end apart: 3 -> 0, of which waited for: 3 -> 0; matrix products, arithmetic and copies ran while one was open for 2% -> 0% of each run, Pallas kernels for 0% -> 0%
where the time goes in v1:
time: 96.2 us; the launch traced here: 95.9 us
  Pallas kernels  92.6 us (96%)
  local copies, waits for them, and re-layouts  3.36 us (3%)
    pallas_call x1, Pallas kernels, fused_device(): pl.pallas_call(fused_kernel, out_shape=jax.ShapeDtypeStruct((rows, column...  92.6 us
    unnamed x2, local copies, waits for them, and re-layouts  3.36 us

profile of v1, /device:TPU:2, one launch (start us, length us, event | category | flops | bytes accessed | tf_op | source)
XLA Modules:
  0.0 95.9 jit_solution(8583365118521544071)
XLA Ops:
  0.0 1.4 %copy.7.bl_ref = s32[80,8]{1,0:T(8,128)} copy(s32[80,8]{0,1:T(8,128)} %param.10) | data formatting | bytes 5120 | tf_op args[4]
  1.4 92.6 %shard_map.64 = bf16[80,4096]{1,0:T(8,128)(2,1)} custom-call(bf16[80,4096]{1,0:T(8,128)(2,1)} %q_ref.1, bf16[10,8,64,256]{3,2,1,0:T(8,128)(2,1)} %kv_ref.1, bf16[4096,4096]{1,0:T(8,128)(2,1)} %w_ref.1, bf16[80,4096]{1,0:T(8,128)(2,1)} %res_ref.1, s32[80,8]{1,0:T(8,128)} %copy.7.bl_ref, s32[1,80]{1,0:T(1,128)} %bitcast.1), custom_call_target="tpu_custom_call" | custom-call | flops 10737418240 | bytes 33554432 | tf_op jit(solution)/shard_map/pallas_call | solution.py:374
  94.0 2.0 %copy.9 = bf16[80,4096]{1,0:T(8,128)(2,1)} copy(bf16[80,4096]{1,0:T(8,128)(2,1)} %shard_map.64) | data formatting | bytes 1310720

commit v2 on v1

--- a/solution.py
+++ b/solution.py
@@ -84,7 +84,7 @@
 
 def fused_kernel(
     q_ref, kv_ref, w_ref, res_ref, bl_ref, len_ref, out_ref,
-    w_v, kvb, kc, vc, bias, ids_v, ids_s, attb, stg, rl, rr, facc,
+    w_v, kvb, kc, vc, ids_v, ids_s, attb, stg, rl, rr, facc,
     w_sem, ids_sem, kvl_sem, kv_send, kv_recv, at_send, at_recv, z_send, zl_recv, zr_recv,
 ):
     rows, width = q_ref.shape
@@ -149,9 +149,6 @@
 
     for t in range(2 * local_kv):
         kv_local(t).start()
-    for j in range(n_col):
-        w_copy(j).start()
-
     barrier = pltpu.get_barrier_semaphore()
     pl.semaphore_signal(barrier, inc=1, device_id={"dp": mate}, device_id_type=MESH)
     pl.semaphore_signal(barrier, inc=1, device_id={"dp": across}, device_id_type=MESH)
@@ -172,18 +169,20 @@
         kv_remote(1, t).start()
     for t in range(2 * local_kv):
         kv_remote(0, t).start()
+    for j in range(n_col):
+        w_copy(j).start()
 
     bl = bl_ref[...]
-    list_len = bl.shape[1]
-    lane = lax.broadcasted_iota(jnp.int32, (rows, 128), 1)
-    hit = jnp.zeros((rows, 128), jnp.int32)
+    list_len = bl.shape[0]
+    sub = lax.broadcasted_iota(jnp.int32, (128, rows), 0)
+    hit = jnp.zeros((128, rows), jnp.int32)
     for k in range(list_len):
-        hit = jnp.maximum(hit, (bl[:, k : k + 1] == lane).astype(jnp.int32))
-    named_l = jnp.max(hit, axis=0, keepdims=True)
+        hit = jnp.maximum(hit, (bl[k : k + 1, :] == sub).astype(jnp.int32))
+    named_s = jnp.max(hit, axis=1, keepdims=True)
     sub2 = lax.broadcasted_iota(jnp.int32, (128, 128), 0)
     lane2 = lax.broadcasted_iota(jnp.int32, (128, 128), 1)
+    named_l = jnp.sum(jnp.where(sub2 == lane2, named_s, 0), axis=0, keepdims=True)
     named_b = jnp.broadcast_to(named_l, (128, 128))
-    named_s = jnp.sum(jnp.where(sub2 == lane2, named_b, 0), axis=1, keepdims=True)
     rank = jnp.sum(jnp.where(lane2 < sub2, named_b, 0), axis=1, keepdims=True)
     picked = jnp.where((rank == lane2) & (named_s > 0), sub2, 0)
     ids = jnp.sum(picked, axis=0, keepdims=True)
@@ -192,22 +191,19 @@
     ids_copy.start()
     ids_copy.wait()
 
-    eye_r = lax.broadcasted_iota(jnp.int32, (rows, rows), 0)
-    eye_c = lax.broadcasted_iota(jnp.int32, (rows, rows), 1)
-    len_b = jnp.broadcast_to(len_ref[...], (rows, rows))
-    length = jnp.sum(jnp.where(eye_r == eye_c, len_b, 0), axis=1, keepdims=True)
-    place = lax.broadcasted_iota(jnp.int32, (rows, list_len), 1)
-    token = lax.broadcasted_iota(jnp.int32, (rows, 2 * blk), 1)
-    for pair_of in range(slots // 2):
-        limits = []
-        for k in range(2):
-            match = bl == ids_s[0, 2 * pair_of + k]
-            left = jnp.where(match, length - place * blk, 0)
-            limits.append(jnp.max(left, axis=1, keepdims=True))
-        limit = jnp.where(token < blk, jnp.minimum(limits[0], blk), limits[1] + blk)
-        bias[:, 2 * blk * pair_of : 2 * blk * (pair_of + 1)] = jnp.where(token < limit, 0.0, -1e30)
-
-    scale = 1.0 / math.sqrt(hd)
+    place = lax.broadcasted_iota(jnp.int32, (list_len, rows), 0)
+    token = lax.broadcasted_iota(jnp.int32, (blk, rows), 0)
+    kc[:, hd:] = jnp.zeros((slots * blk, hd), jnp.bfloat16)
+    for k in range(slots):
+        left = jnp.where(bl == ids_s[0, k], len_ref[...] - place * blk, 0)
+        limit = jnp.max(left, axis=0, keepdims=True)
+        mask = jnp.where(token < limit, 0.0, -1e30).astype(jnp.bfloat16)
+        kc[blk * k : blk * (k + 1), hd : hd + rows] = mask
+    vc[:, hd:] = jnp.ones((slots * blk, hd), jnp.bfloat16)
+    row_of = lax.broadcasted_iota(jnp.int32, (rows, hd), 0)
+    own_row = (row_of == lax.broadcasted_iota(jnp.int32, (rows, hd), 1)).astype(jnp.bfloat16)
+
+    scale = math.log2(math.e) / math.sqrt(hd)
     for h in range(local_kv):
         for t in (2 * h, 2 * h + 1):
             kv_remote(1, t).wait_recv()
@@ -218,8 +214,8 @@
             kv_remote(2, t).wait_recv()
         for j in range(slots):
             pick = ids_s[0, j]
-            kc[blk * j : blk * (j + 1), :] = kvb[2 * h][pick]
-            vc[blk * j : blk * (j + 1), :] = kvb[2 * h + 1][pick]
+            kc[blk * j : blk * (j + 1), :hd] = kvb[2 * h][pick]
+            vc[blk * j : blk * (j + 1), :hd] = kvb[2 * h + 1][pick]
 
         @pl.loop(0, groups_per_kv)
         def _(g):
@@ -227,20 +223,19 @@
             cols = pl.ds(pl.multiple_of(i * CHUNK, CHUNK), CHUNK)
             qs = q_ref[:, cols]
             stacked = jnp.concatenate(
-                [qs[:, hd * k : hd * (k + 1)] for k in range(per)], axis=0
+                [
+                    jnp.concatenate([qs[:, hd * k : hd * (k + 1)], own_row], axis=1)
+                    for k in range(per)
+                ],
+                axis=0,
             )
             scores = lax.dot_general(
                 stacked, kc[...], (((1,), (1,)), ((), ())), preferred_element_type=jnp.float32
-            ).reshape(per, rows, slots * blk)
-            scores = scores * scale + bias[...][None]
-            top = jnp.max(scores, axis=2, keepdims=True)
-            weights = jnp.exp(scores - top)
-            total = jnp.sum(weights, axis=2, keepdims=True)
-            summed = jnp.dot(
-                weights.astype(jnp.bfloat16).reshape(per * rows, slots * blk),
-                vc[...], preferred_element_type=jnp.float32,
-            ).reshape(per, rows, hd)
-            attended = (summed / total).astype(jnp.bfloat16)
+            )
+            top = jnp.max(scores, axis=1, keepdims=True)
+            weights = jnp.exp2((scores - top) * scale).astype(jnp.bfloat16)
+            summed = jnp.dot(weights, vc[...], preferred_element_type=jnp.float32)
+            attended = (summed[:, :hd] / summed[:, hd:]).astype(jnp.bfloat16).reshape(per, rows, hd)
             attb[d, :, cols] = jnp.concatenate([attended[k] for k in range(per)], axis=1)
             att_remote(1, i).start()
             att_remote(0, i).start()
@@ -291,8 +286,7 @@
             def _():
                 pass_on(b, False)
 
-    @pl.loop(0, 2 * n_col)
-    def _(s):
+    def project(s):
         j = s % n_col
         cols = pl.ds(pl.multiple_of(j * CHUNK, CHUNK), CHUNK)
 
@@ -314,11 +308,21 @@
         stg[pl.ds(2 * chip, 2), :, cols] = partial.astype(jnp.bfloat16).reshape(2, rows, CHUNK)
         send_end(s)
 
-        @pl.when(s > 0)
-        def _():
-            send_inner(s - 1)
-
-    send_inner(2 * n_col - 1)
+    lag = n_col // 2
+
+    @pl.loop(0, n_col + lag)
+    def _(m):
+        @pl.when(m < n_col)
+        def _():
+            @pl.loop(2 * m, 2 * m + 2)
+            def _(s):
+                project(s)
+
+            send_inner(m)
+
+        @pl.when(m >= lag)
+        def _():
+            send_inner(n_col + m - lag)
 
     @pl.loop(0, n_col)
     def _(j):
@@ -379,9 +383,8 @@
         scratch_shapes=[
             pltpu.VMEM((n_col, width, CHUNK), bf16),
             [pltpu.VMEM((n_dp * stores, blk, hd), bf16)] * (2 * local_kv),
-            pltpu.VMEM((tokens, hd), bf16),
-            pltpu.VMEM((tokens, hd), bf16),
-            pltpu.VMEM((rows, tokens), f32),
+            pltpu.VMEM((tokens, 2 * hd), bf16),
+            pltpu.VMEM((tokens, 2 * hd), bf16),
             pltpu.VMEM((8, 128), jnp.int32),
             pltpu.SMEM((8, 128), jnp.int32),
             pltpu.VMEM((n_dp, rows, width), bf16),
@@ -408,7 +411,7 @@
             bytes_accessed=2 * width * columns,
             transcendentals=rows * width // hd * tokens,
         ),
-    )(queries, kv_pool, out_weight, residual, block_lists, lengths.reshape(1, rows))
+    )(queries, kv_pool, out_weight, residual, block_lists.T, lengths.reshape(1, rows))
 
 
 def fits_fused(mesh):

time: 96.2 us -> 97.5 us (1.014)
  Pallas kernels: 92.6 us -> 95.3 us
  local copies, waits for them, and re-layouts: 3.36 us -> 1.97 us
    pallas_call x1, Pallas kernels: 92.6 us -> 95.3 us  [fused_device(): pl.pallas_call(fused_kernel, out_shape=jax.ShapeDtypeStruct((rows, column...]
    unnamed x2 -> x1, local copies, waits for them, and re-layouts: 3.36 us -> 1.97 us
where the time goes in v2:
time: 97.5 us; the launch traced here: 97.3 us
  Pallas kernels  95.3 us (98%)
  local copies, waits for them, and re-layouts  1.97 us (2%)
    pallas_call x1, Pallas kernels, fused_device(): pl.pallas_call(fused_kernel, out_shape=jax.ShapeDtypeStruct((rows, column...  95.3 us
    unnamed x1, local copies, waits for them, and re-layouts  1.97 us

profile of v2, /device:TPU:2, one launch (start us, length us, event | category | flops | bytes accessed | tf_op | source)
XLA Modules:
  0.0 97.3 jit_solution(1204334124140159351)
XLA Ops:
  0.0 95.3 %shard_map.64 = bf16[80,4096]{1,0:T(8,128)(2,1)} custom-call(bf16[80,4096]{1,0:T(8,128)(2,1)} %q_ref.1, bf16[10,8,64,256]{3,2,1,0:T(8,128)(2,1)} %kv_ref.1, bf16[4096,4096]{1,0:T(8,128)(2,1)} %w_ref.1, bf16[80,4096]{1,0:T(8,128)(2,1)} %res_ref.1, s32[8,80]{1,0:T(8,128)} %bitcast.2, s32[1,80]{1,0:T(1,128)} %bitcast.3), custom_call_target="tpu_custom_call" | custom-call | flops 10737418240 | bytes 33554432 | tf_op jit(solution)/shard_map/pallas_call | solution.py:378
  95.3 2.0 %copy.8 = bf16[80,4096]{1,0:T(8,128)(2,1)} copy(bf16[80,4096]{1,0:T(8,128)(2,1)} %shard_map.64) | data formatting | bytes 1310720

commit v3 on v2

--- a/solution.py
+++ b/solution.py
@@ -165,7 +165,7 @@
         barrier, 2 + (z > 0).astype(jnp.int32) + (z < nz - 1).astype(jnp.int32)
     )
 
-    for t in range(2 * local_kv):
+    for t in range(2):
         kv_remote(1, t).start()
     for t in range(2 * local_kv):
         kv_remote(0, t).start()
@@ -206,8 +206,15 @@
     scale = math.log2(math.e) / math.sqrt(hd)
     for h in range(local_kv):
         for t in (2 * h, 2 * h + 1):
+            kv_remote(1, t).wait_send()
+            if h + 1 < local_kv:
+                kv_remote(1, t + 2).start()
+        for t in (2 * h, 2 * h + 1):
             kv_remote(1, t).wait_recv()
             kv_remote(2, t).start()
+        if h + 1 == local_kv:
+            for i in range(h * groups_per_kv):
+                att_remote(1, i).start()
         for t in (2 * h, 2 * h + 1):
             kv_local(t).wait()
             kv_remote(0, t).wait_recv()
@@ -237,7 +244,8 @@
             summed = jnp.dot(weights, vc[...], preferred_element_type=jnp.float32)
             attended = (summed[:, :hd] / summed[:, hd:]).astype(jnp.bfloat16).reshape(per, rows, hd)
             attb[d, :, cols] = jnp.concatenate([attended[k] for k in range(per)], axis=1)
-            att_remote(1, i).start()
+            if h + 1 == local_kv:
+                att_remote(1, i).start()
             att_remote(0, i).start()
 
     @pl.loop(0, n_att)
@@ -246,23 +254,32 @@
 
     inner = (z > 0) & (z < nz - 1)
     half = nz // 2
+    ahead = 2
+    spread = n_att // (n_col // 2)
 
     def block_of(s, i):
         chip = jnp.where(s < n_col, x, 1 - x)
         return 2 * chip + jnp.where(z < half, 1 - i, i)
 
-    def send_end(s):
+    def at_end(s, act):
         j = s % n_col
         for i in range(2):
             b = block_of(s, i)
 
             @pl.when((z == 0) & (b > 0))
             def _():
-                z_remote(b, j, True).start()
+                act(z_remote(b, j, True))
 
             @pl.when((z == nz - 1) & (b < nz - 1))
             def _():
-                z_remote(b, j, False).start()
+                act(z_remote(b, j, False))
+
+    def send_end(s):
+        @pl.when(s >= ahead)
+        def _():
+            at_end(s - ahead, lambda copy: copy.wait_send())
+
+        at_end(s, lambda copy: copy.start())
 
     def send_inner(s):
         j = s % n_col
@@ -293,8 +310,13 @@
         @pl.when(s < n_col)
         def _():
             w_copy(j).wait()
-            att_remote(1, j).wait_recv()
-            att_remote(2, j).start()
+
+        @pl.when((s >= n_col // 2) & (s < n_col))
+        def _():
+            for k in range(spread):
+                i = (j - n_col // 2) * spread + k
+                att_remote(1, i).wait_recv()
+                att_remote(2, i).start()
 
         @pl.when(s == n_col)
         def _():
@@ -342,22 +364,26 @@
         out_ref[:, cols] = facc[...].astype(jnp.bfloat16)
 
     for kind in range(3):
-        for t in range(2 * local_kv):
-            kv_remote(kind, t).wait_send()
+        if kind != 1:
+            for t in range(2 * local_kv):
+                kv_remote(kind, t).wait_send()
 
         @pl.loop(0, n_att)
         def _(i):
             att_remote(kind, i).wait_send()
 
+    for s in range(2 * n_col - ahead, 2 * n_col):
+        at_end(s, lambda copy: copy.wait_send())
+
     @pl.loop(0, n_col)
     def _(j):
         for b in range(nz):
 
-            @pl.when(z < b)
+            @pl.when(inner & (z < b))
             def _():
                 z_remote(b, j, True).wait_send()
 
-            @pl.when(z > b)
+            @pl.when(inner & (z > b))
             def _():
                 z_remote(b, j, False).wait_send()
 

time: 97.5 us -> 96.7 us (level)
  no operation moved by 1% of the time
where the time goes in v3:
time: 96.7 us; the launch traced here: 96.4 us
  Pallas kernels  94.5 us (98%)
  local copies, waits for them, and re-layouts  1.97 us (2%)
    pallas_call x1, Pallas kernels, fused_device(): pl.pallas_call(fused_kernel, out_shape=jax.ShapeDtypeStruct((rows, column...  94.5 us
    unnamed x1, local copies, waits for them, and re-layouts  1.97 us

profile of v3, /device:TPU:2, one launch (start us, length us, event | category | flops | bytes accessed | tf_op | source)
XLA Modules:
  0.0 96.4 jit_solution(14842166395102271333)
XLA Ops:
  0.0 94.5 %shard_map.64 = bf16[80,4096]{1,0:T(8,128)(2,1)} custom-call(bf16[80,4096]{1,0:T(8,128)(2,1)} %q_ref.1, bf16[10,8,64,256]{3,2,1,0:T(8,128)(2,1)} %kv_ref.1, bf16[4096,4096]{1,0:T(8,128)(2,1)} %w_ref.1, bf16[80,4096]{1,0:T(8,128)(2,1)} %res_ref.1, s32[8,80]{1,0:T(8,128)} %bitcast.2, s32[1,80]{1,0:T(1,128)} %bitcast.3), custom_call_target="tpu_custom_call" | custom-call | flops 10737418240 | bytes 33554432 | tf_op jit(solution)/shard_map/pallas_call | solution.py:404
  94.5 2.0 %copy.8 = bf16[80,4096]{1,0:T(8,128)(2,1)} copy(bf16[80,4096]{1,0:T(8,128)(2,1)} %shard_map.64) | data formatting | bytes 1310720

commit v4 on v3

--- a/solution.py
+++ b/solution.py
@@ -281,27 +281,23 @@
 
         at_end(s, lambda copy: copy.start())
 
-    def send_inner(s):
-        j = s % n_col
-        cols = pl.ds(pl.multiple_of(j * CHUNK, CHUNK), CHUNK)
-
-        def pass_on(b, right):
+    skew = 2
+
+    def send_inner(first, m):
+        for right in (True, False):
+            j = m - skew * (z - 1 if right else nz - 2 - z)
+            cols = pl.ds(pl.multiple_of(j * CHUNK, CHUNK), CHUNK)
             land = rl if right else rr
-            z_remote(b, j, right).wait_recv()
-            added = stg[b, :, cols].astype(jnp.float32) + land[b, :, cols].astype(jnp.float32)
-            stg[b, :, cols] = added.astype(jnp.bfloat16)
-            z_remote(b, j, right).start()
-
-        for i in range(2):
-            b = block_of(s, i)
-
-            @pl.when(inner & (b > z))
-            def _():
-                pass_on(b, True)
-
-            @pl.when(inner & (b < z))
-            def _():
-                pass_on(b, False)
+            for i in range(2):
+                b = block_of(first, i)
+
+                @pl.when(inner & (j >= 0) & (j < n_col) & (b > z if right else b < z))
+                def _():
+                    z_remote(b, j, right).wait_recv()
+                    own = stg[b, :, cols].astype(jnp.float32)
+                    added = own + land[b, :, cols].astype(jnp.float32)
+                    stg[b, :, cols] = added.astype(jnp.bfloat16)
+                    z_remote(b, j, right).start()
 
     def project(s):
         j = s % n_col
@@ -332,7 +328,7 @@
 
     lag = n_col // 2
 
-    @pl.loop(0, n_col + lag)
+    @pl.loop(0, n_col + lag + skew * (nz - 3))
     def _(m):
         @pl.when(m < n_col)
         def _():
@@ -340,11 +336,8 @@
             def _(s):
                 project(s)
 
-            send_inner(m)
-
-        @pl.when(m >= lag)
-        def _():
-            send_inner(n_col + m - lag)
+        send_inner(0, m)
+        send_inner(n_col, m - lag)
 
     @pl.loop(0, n_col)
     def _(j):

time: 96.7 us -> 82.5 us (0.85)
  Pallas kernels: 94.5 us -> 80.3 us
    pallas_call x1, Pallas kernels: 94.5 us -> 80.3 us  [fused_device(): pl.pallas_call(fused_kernel, out_shape=jax.ShapeDtypeStruct((rows, column...]
where the time goes in v4:
time: 82.5 us; the launch traced here: 82.3 us
  Pallas kernels  80.3 us (97%)
  local copies, waits for them, and re-layouts  1.97 us (2%)
    pallas_call x1, Pallas kernels, fused_device(): pl.pallas_call(fused_kernel, out_shape=jax.ShapeDtypeStruct((rows, column...  80.3 us
    unnamed x1, local copies, waits for them, and re-layouts  1.97 us

profile of v4, /device:TPU:2, one launch (start us, length us, event | category | flops | bytes accessed | tf_op | source)
XLA Modules:
  0.0 82.3 jit_solution(17395828585660629954)
XLA Ops:
  0.0 80.3 %shard_map.64 = bf16[80,4096]{1,0:T(8,128)(2,1)} custom-call(bf16[80,4096]{1,0:T(8,128)(2,1)} %q_ref.1, bf16[10,8,64,256]{3,2,1,0:T(8,128)(2,1)} %kv_ref.1, bf16[4096,4096]{1,0:T(8,128)(2,1)} %w_ref.1, bf16[80,4096]{1,0:T(8,128)(2,1)} %res_ref.1, s32[8,80]{1,0:T(8,128)} %bitcast.2, s32[1,80]{1,0:T(1,128)} %bitcast.3), custom_call_target="tpu_custom_call" | custom-call | flops 10737418240 | bytes 33554432 | tf_op jit(solution)/shard_map/pallas_call | solution.py:397
  80.3 2.0 %copy.8 = bf16[80,4096]{1,0:T(8,128)(2,1)} copy(bf16[80,4096]{1,0:T(8,128)(2,1)} %shard_map.64) | data formatting | bytes 1310720

commit v5 on v4

--- a/solution.py
+++ b/solution.py
@@ -254,7 +254,7 @@
 
     inner = (z > 0) & (z < nz - 1)
     half = nz // 2
-    ahead = 2
+    ahead = 3
     spread = n_att // (n_col // 2)
 
     def block_of(s, i):
@@ -281,7 +281,7 @@
 
         at_end(s, lambda copy: copy.start())
 
-    skew = 2
+    skew = 3
 
     def send_inner(first, m):
         for right in (True, False):

time: 82.5 us -> 82.5 us (level)
  no operation moved by 1% of the time
where the time goes in v5:
time: 82.5 us; the launch traced here: 82.3 us
  Pallas kernels  80.3 us (97%)
  local copies, waits for them, and re-layouts  1.97 us (2%)
    pallas_call x1, Pallas kernels, fused_device(): pl.pallas_call(fused_kernel, out_shape=jax.ShapeDtypeStruct((rows, column...  80.3 us
    unnamed x1, local copies, waits for them, and re-layouts  1.97 us

profile of v5, /device:TPU:2, one launch (start us, length us, event | category | flops | bytes accessed | tf_op | source)
XLA Modules:
  0.0 82.3 jit_solution(1670466256741296303)
XLA Ops:
  0.0 80.3 %shard_map.64 = bf16[80,4096]{1,0:T(8,128)(2,1)} custom-call(bf16[80,4096]{1,0:T(8,128)(2,1)} %q_ref.1, bf16[10,8,64,256]{3,2,1,0:T(8,128)(2,1)} %kv_ref.1, bf16[4096,4096]{1,0:T(8,128)(2,1)} %w_ref.1, bf16[80,4096]{1,0:T(8,128)(2,1)} %res_ref.1, s32[8,80]{1,0:T(8,128)} %bitcast.2, s32[1,80]{1,0:T(1,128)} %bitcast.3), custom_call_target="tpu_custom_call" | custom-call | flops 10737418240 | bytes 33554432 | tf_op jit(solution)/shard_map/pallas_call | solution.py:397
  80.3 2.0 %copy.8 = bf16[80,4096]{1,0:T(8,128)(2,1)} copy(bf16[80,4096]{1,0:T(8,128)(2,1)} %shard_map.64) | data formatting | bytes 1310720
